TPU v7x, 32 devices: a whole 2x2x4 slice. The times are simulated.
32 devices in a mesh: parts: 2 (over x), seq: 8 (over z, y), head: 2 (over core).
Axes of the slice: x: 2, y: 2, z: 4, core: 2. Of those that a mesh axis runs over, the one named last changes fastest.
Arguments:
- queries: bfloat16 [8192, 2048], P(('parts', 'seq', 'head')), parts along dimension 0, may hold values from -6 to 6
- keys: bfloat16 [8192, 2048], P(('parts', 'seq', 'head')), parts along dimension 0, may hold values from -6 to 6
- values: bfloat16 [8192, 2048], P(('parts', 'seq', 'head')), parts along dimension 0, may hold values from -25 to 25
- out_grad: bfloat16 [8192, 2048], P(('parts', 'seq', 'head')), parts along dimension 0, may hold values from -6 to 6
- log_decay: bfloat16 [8192, 16], P(('parts', 'seq', 'head')), parts along dimension 0, may hold values from -1.6 to 0, as said below
Outputs:
- out: bfloat16 [8192, 2048], P(('parts', 'seq', 'head')), parts along dimension 0
- query_grad: bfloat16 [8192, 2048], P(('parts', 'seq', 'head')), parts along dimension 0
- key_grad: bfloat16 [8192, 2048], P(('parts', 'seq', 'head')), parts along dimension 0
- value_grad: bfloat16 [8192, 2048], P(('parts', 'seq', 'head')), parts along dimension 0
There are 2 independent parts, one for each index of `parts`. A program takes and returns all parts, laid end to end along the dimension named above; each array names one. Nothing has to cross between parts.
Inputs may be any that keep to these rules, and one draw needn't show every extreme that they name: `log_decay`: strictly negative.
All inputs are finite; a program needn't handle non-finite values.
Results may differ from a plain program's by a relative error of at most 0.0053.
Values may be sent and summed in bfloat16 or wider, within the bound.
A program may use at most 128 MiB of HBM per device.

v0:
```python
import jax
import jax.numpy as jnp
from jax import lax
from jax.sharding import PartitionSpec as P

DH = 128
BLOCK = 256


EPSILON = 1e-06
highest = lax.Precision.HIGHEST


def entering(part, axis, combine, identity, reverse):
    count = lax.axis_size(axis)
    place = lax.axis_index(axis)
    ahead = count - 1 - place if reverse else place
    gathered = jax.tree.map(lambda a: lax.all_gather(a, axis), part)
    state = jax.tree.map(lambda a, e: jnp.zeros_like(a) + jnp.asarray(e, a.dtype), part, identity)

    def one(lap, state):
        source = count - 1 - lap if reverse else lap
        return combine(
            state, jax.tree.map(lambda a: lax.dynamic_index_in_dim(a, source, 0, False), gathered)
        )

    return lax.fori_loop(0, ahead, one, state)


def decay_weights(within_b):
    size = within_b.shape[0]
    index = jnp.arange(size)
    lower = index[:, None] >= index[None, :]
    spread = within_b.T[:, :, None] - within_b.T[:, None, :]
    return jnp.where(lower[None], jnp.exp(jnp.minimum(spread, 0.0)), 0.0)


def combine_states(earlier, later):
    return (earlier[0] + later[0], jnp.exp(later[0])[:, None, None] * earlier[1] + later[1])


def body(queries, keys, values, out_grad, log_decay):
    query_rows, key_rows, value_rows, cotan_rows, decay_rows = (
        lax.all_to_all(queries, "head", split_axis=1, concat_axis=0, tiled=True),
        lax.all_to_all(keys, "head", split_axis=1, concat_axis=0, tiled=True),
        lax.all_to_all(values, "head", split_axis=1, concat_axis=0, tiled=True),
        lax.all_to_all(out_grad, "head", split_axis=1, concat_axis=0, tiled=True),
        lax.all_to_all(log_decay, "head", split_axis=1, concat_axis=0, tiled=True),
    )
    rows = query_rows.shape[0]
    heads = query_rows.shape[1] // DH
    blocks = rows // BLOCK
    shape4 = (blocks, BLOCK, heads, DH)
    query_blocks = query_rows.reshape(shape4)
    key_blocks = key_rows.reshape(shape4)
    value_blocks = value_rows.reshape(shape4)
    within = jnp.cumsum(decay_rows.astype(jnp.float32).reshape(blocks, BLOCK, heads), axis=1)
    totals = within[:, -1, :]
    fading = jnp.exp(totals[:, None, :] - within)
    growing = jnp.exp(within)
    local = jnp.einsum(
        "jshd,jshe->jhde",
        key_blocks.astype(jnp.float32) * fading[..., None],
        value_blocks.astype(jnp.float32),
        precision=highest,
    )
    blank = jnp.zeros((heads, DH, DH), jnp.float32)
    zero_heads = jnp.zeros((heads,), jnp.float32)

    def carry_state(state, piece):
        return (jnp.exp(piece[0])[:, None, None] * state + piece[1], state)

    span_state, entering_local_state = lax.scan(carry_state, blank, (totals, local))
    span_total = jnp.sum(totals, axis=0)
    start_total, start_state = entering(
        (span_total, span_state), "seq", combine_states, (zero_heads, blank), False
    )
    before = jnp.cumsum(totals, axis=0) - totals
    enter = jnp.exp(before)[:, :, None, None] * start_state[None] + entering_local_state

    def forward_block(piece):
        query_b, key_b, value_b, within_b, enter_b = piece
        weights = decay_weights(within_b)
        scores = (
            jnp.einsum("thd,shd->hts", query_b, key_b, preferred_element_type=jnp.float32) * weights
        )
        cross = jnp.einsum("thd,hde->the", query_b.astype(jnp.float32), enter_b, precision=highest)
        intra = jnp.einsum(
            "hts,she->the", scores.astype(jnp.bfloat16), value_b, preferred_element_type=jnp.float32
        )
        return intra + jnp.exp(within_b)[:, :, None] * cross

    numer = lax.map(forward_block, (query_blocks, key_blocks, value_blocks, within, enter))
    scale = jnp.sqrt(jnp.mean(numer * numer, axis=-1, keepdims=True) + EPSILON)
    normed = numer / scale
    out_rows = normed.astype(jnp.bfloat16).reshape(rows, heads * DH)
    cotan = cotan_rows.reshape(shape4).astype(jnp.float32)
    grad_num = (cotan - normed * jnp.mean(cotan * normed, axis=-1, keepdims=True)) / scale
    hterm = jnp.einsum(
        "jthd,jthe->jhde",
        query_blocks.astype(jnp.float32) * growing[..., None],
        grad_num,
        precision=highest,
    )

    def carry_grad(state, piece):
        return (piece[1] + jnp.exp(piece[0])[:, None, None] * state, state)

    span_grad, back_local = lax.scan(carry_grad, blank, (totals, hterm), reverse=True)
    later_total, start_grad = entering(
        (span_total, span_grad), "seq", combine_states, (zero_heads, blank), True
    )
    after = span_total[None] - jnp.cumsum(totals, axis=0)
    back = jnp.exp(after)[:, :, None, None] * start_grad[None] + back_local

    def backward_block(piece):
        query_b, key_b, value_b, within_b, enter_b, back_b, grad_b = piece
        weights = decay_weights(within_b)
        scores = (
            jnp.einsum("thd,shd->hts", query_b, key_b, preferred_element_type=jnp.float32) * weights
        )
        grad_short = grad_b.astype(jnp.bfloat16)
        mixed = (
            jnp.einsum("the,she->hts", grad_short, value_b, preferred_element_type=jnp.float32)
            * weights
        ).astype(jnp.bfloat16)
        fade_b = jnp.exp(within_b[-1][None, :] - within_b)[:, :, None]
        query_grad = jnp.einsum(
            "hts,shd->thd", mixed, key_b, preferred_element_type=jnp.float32
        ) + jnp.exp(within_b)[:, :, None] * jnp.einsum(
            "the,hde->thd", grad_b, enter_b, precision=highest
        )
        key_grad = jnp.einsum(
            "hts,thd->shd", mixed, query_b, preferred_element_type=jnp.float32
        ) + fade_b * jnp.einsum(
            "she,hde->shd", value_b.astype(jnp.float32), back_b, precision=highest
        )
        value_grad = jnp.einsum(
            "hts,the->she",
            scores.astype(jnp.bfloat16),
            grad_short,
            preferred_element_type=jnp.float32,
        ) + fade_b * jnp.einsum(
            "shd,hde->she", key_b.astype(jnp.float32), back_b, precision=highest
        )
        return (
            query_grad.astype(jnp.bfloat16),
            key_grad.astype(jnp.bfloat16),
            value_grad.astype(jnp.bfloat16),
        )

    query_grad, key_grad, value_grad = lax.map(
        backward_block, (query_blocks, key_blocks, value_blocks, within, enter, back, grad_num)
    )
    flat = (rows, heads * DH)
    query_flat = query_grad.reshape(flat)
    key_flat = key_grad.reshape(flat)
    flattened_values = value_grad.reshape(flat)
    out_tokens, query_tokens, token_key_rows, value_tokens = (
        lax.all_to_all(out_rows, "head", split_axis=0, concat_axis=1, tiled=True),
        lax.all_to_all(query_flat, "head", split_axis=0, concat_axis=1, tiled=True),
        lax.all_to_all(key_flat, "head", split_axis=0, concat_axis=1, tiled=True),
        lax.all_to_all(flattened_values, "head", split_axis=0, concat_axis=1, tiled=True),
    )
    return (out_tokens, query_tokens, token_key_rows, value_tokens)


def solution(mesh):
    placed = (
        P(("parts", "seq", "head"), None),
        P(("parts", "seq", "head"), None),
        P(("parts", "seq", "head"), None),
        P(("parts", "seq", "head"), None),
        P(("parts", "seq", "head"), None),
    )
    return jax.shard_map(
        body,
        mesh=mesh,
        in_specs=placed,
        out_specs=(
            P(("parts", "seq", "head"), None),
            P(("parts", "seq", "head"), None),
            P(("parts", "seq", "head"), None),
            P(("parts", "seq", "head"), None),
        ),
        check_vma=False,
    )
```

profile of v0, /device:TPU:0, one launch (start us, length us, event | category | flops | bytes accessed | tf_op | source)
XLA Modules:
  0.0 298.1 jit_solution(4400105236584361990)
XLA Ops:
  7.2 3.2 %all-to-all-start.3 = ((bf16[256,2,8]{0,2,1:T(8,128)(2,1)}), bf16[256,2,8]{0,2,1:T(8,128)(2,1)S(1)}, u32[]{:S(2)}, u32[]{:S(2)}) async-start(bf16[256,2,8]{0,2,1:T(8,128)(2,1)} %bitcast.318), calls=%async_computation.3 | async-start | bytes 16384 | tf_op jit(solution)/shard_map/all_to_all | solution.py:48
  10.4 2.4 copy.88
  12.8 3.6 %all-to-all-start = ((bf16[256,2,1024]{0,2,1:T(8,128)(2,1)}), bf16[256,2,1024]{0,2,1:T(8,128)(2,1)S(1)}, u32[]{:S(2)}, u32[]{:S(2)}) async-start(bf16[256,2,1024]{0,2,1:T(8,128)(2,1)} %bitcast.32), calls=%async_computation | async-start | bytes 2097152 | tf_op jit(solution)/shard_map/all_to_all | solution.py:46
  16.4 1.2 reduce-window.6
  18.2 1.3 copy.117
  19.5 5.7 %all_to_all.150 = bf16[256,2,1024]{0,2,1:T(8,128)(2,1)S(1)} all-to-all(bf16[256,2,1024]{0,2,1:T(8,128)(2,1)} %bitcast.307), channel_id=1, replica_groups=mesh['parts'=2,'seq'=8,'head'=2] {'head'}, dimensions={1} | all-to-all | bytes 2097152 | tf_op jit(solution)/shard_map/all_to_all | solution.py:45
  25.2 2.2 fusion.91
  27.3 1.1 broadcast.69.clone
  28.4 4.0 %while.84 = (s32[]{:T(128)}, f32[8,128,128]{2,1,0:T(8,128)S(1)}, f32[2,8,128,128]{3,2,1,0:T(8,128)}, f32[2,8]{1,0:T(2,128)S(1)}, f32[2,8,128,128]{3,2,1,0:T(8,128)}, /*index=5*/s32[]{:T(128)}, s32[]{:T(128)}) while((s32[]{:T(128)}, f32[8,128,128]{2,1,0:T(8,128)S(1)}, f32[2,8,128,128]{3,2,1,0:T(8,128)}, f32[2,8]{1,0:T(2,128)S(1)}, ...), condition=%wide.region_5.6_spmd.clone, body=%wide.region_4.5_spmd.clone.sunk | while | flops 524291 | bytes 2622144 | solution.py:73
  29.2 1.2 bitcast_add_fusion.10
  31.3 1.2 bitcast_add_fusion.10
  33.3 1.3 copy.116
  34.6 4.6 %all-to-all-start.1 = ((bf16[256,2,1024]{0,2,1:T(8,128)(2,1)}), bf16[256,2,1024]{0,2,1:T(8,128)(2,1)}, u32[]{:S(2)}, u32[]{:S(2)}) async-start(bf16[256,2,1024]{0,2,1:T(8,128)(2,1)} %bitcast.35), calls=%async_computation.1 | async-start | bytes 2097152 | tf_op jit(solution)/shard_map/all_to_all | solution.py:44
  40.7 23.6 %all-reduce = f32[64]{0:T(128)S(1)} all-reduce(f32[64]{0:T(128)S(1)} %dynamic-update-slice), channel_id=2, replica_groups=mesh['parts'=2,'seq'=8,'head'=2] {'seq'}, use_global_device_ids=true, to_apply=%add | all-reduce | flops 64 | bytes 512
  64.4 1.3 copy.95
  65.7 44.1 %all-gather.6.cloned.1.call-done = f32[64,128,128]{2,1,0:T(8,128)} async-done(((f32[8,128,128]{2,1,0:T(8,128)}), f32[64,128,128]{2,1,0:T(8,128)}) %all-gather.6.cloned.1.call-update) | async-done | bytes 4194320 | tf_op jit(solution)/shard_map/all_gather | solution.py:18
  109.9 1.4 multiply_add_fusion.1
  111.3 4.4 %all-to-all-start.5 = ((bf16[256,2,1024]{0,2,1:T(8,128)(2,1)}), bf16[256,2,1024]{0,2,1:T(8,128)(2,1)}, u32[]{:S(2)}, u32[]{:S(2)}) async-start(bf16[256,2,1024]{0,2,1:T(8,128)(2,1)} %bitcast.306), calls=%async_computation.5 | async-start | bytes 2097152 | tf_op jit(solution)/shard_map/all_to_all | solution.py:47
  115.8 12.4 %while.81 = (s32[]{:T(128)}, f32[2,256,8,128]{1,3,2,0:T(8,128)}, bf16[2,256,8,128]{1,3,2,0:T(8,128)(2,1)}, bf16[2,256,8,128]{1,3,2,0:T(8,128)(2,1)}, bf16[2,256,...) while((s32[]{:T(128)}, f32[2,256,8,128]{1,3,2,0:T(8,128)}, ...), condition=%wide.region_9.10_spmd, body=%wide.region_8.9_spmd.sunk | while | flops 674299904 | bytes 5958749 | solution.py:93
  115.8 2.6 fusion.134
  118.5 3.5 %fusion.135 = f32[2,256,8,128]{1,3,2,0:T(8,128)} fusion(f32[2,256,8,128]{1,3,2,0:T(8,128)} %get-tuple-element.881, s32[]{:T(128)} %get-tuple-element.880, f32[256,8,128]{0,2,1:T(8,128)} %fusion.134, f32[8,256]{1,0:T(8,128)S(1)} %dynamic-slice_bitcast_fusion.4, pred[256,256]{1,0:T(8,128)(4,1)S(1)} %iota_compare_fusion.4, ...), kind=kOutput, calls=%fused_computation.7.clone.1 | convolution fusion | flops 271319040 | bytes 3753984 | tf_op jit(solution)/shard_map/while/body/eval_jaxpr/hts,she->the/dot_general | solution.py:88
  122.0 2.6 fusion.134
  124.7 3.5 %fusion.135 = f32[2,256,8,128]{1,3,2,0:T(8,128)} fusion(f32[2,256,8,128]{1,3,2,0:T(8,128)} %get-tuple-element.881, s32[]{:T(128)} %get-tuple-element.880, f32[256,8,128]{0,2,1:T(8,128)} %fusion.134, f32[8,256]{1,0:T(8,128)S(1)} %dynamic-slice_bitcast_fusion.4, pred[256,256]{1,0:T(8,128)(4,1)S(1)} %iota_compare_fusion.4, ...), kind=kOutput, calls=%fused_computation.7.clone.1 | convolution fusion | flops 271319040 | bytes 3753984 | tf_op jit(solution)/shard_map/while/body/eval_jaxpr/hts,she->the/dot_general | solution.py:88
  128.2 2.5 multiply_reduce_fusion.1
  130.7 2.4 multiply_reduce_fusion
  133.2 2.7 subtract_divide_fusion
  135.9 4.4 %fusion.88 = f32[2,8,128,128]{3,2,1,0:T(8,128)} fusion(f32[2,256,8,128]{1,3,2,0:T(8,128)S(1)} %get-tuple-element.949, bf16[2,256,8,128]{1,3,2,0:T(8,128)(2,1)} %bitcast.37, f32[2,256,8]{1,2,0:T(8,128)S(1)} %get-tuple-element.579), kind=kOutput, calls=%fused_computation.108 | convolution fusion | flops 806354944 | bytes 4210688 | tf_op jit(solution)/shard_map/jthd,jthe->jhde/dot_general | solution.py:99
  140.3 1.1 broadcast.69
  141.4 4.1 %while.85 = (s32[]{:T(128)}, f32[8,128,128]{2,1,0:T(8,128)S(1)}, f32[2,8,128,128]{3,2,1,0:T(8,128)}, f32[2,8,128,128]{3,2,1,0:T(8,128)}, f32[2,8]{1,0:T(2,128)S(1)}, /*index=5*/s32[]{:T(128)}, s32[]{:T(128)}) while((s32[]{:T(128)}, f32[8,128,128]{2,1,0:T(8,128)S(1)}, f32[2,8,128,128]{3,2,1,0:T(8,128)}, ...), condition=%wide.region_13.14_spmd.clone, body=%wide.region_12.13_spmd.clone.sunk | while | flops 524292 | bytes 2621648 | solution.py:109
  142.3 1.2 bitcast_add_fusion.11
  144.3 1.2 bitcast_add_fusion.11
  146.3 5.7 %all_to_all.151 = bf16[2,256,1024]{1,2,0:T(8,128)(2,1)S(1)} all-to-all(bf16[2,256,1024]{1,2,0:T(8,128)(2,1)} %bitcast.312), channel_id=1, replica_groups=mesh['parts'=2,'seq'=8,'head'=2] {'head'}, dimensions={0} | all-to-all | bytes 2097152 | tf_op jit(solution)/shard_map/all_to_all | solution.py:160
  152.0 1.4 copy.105
  153.4 73.3 %all-gather.8.cloned.1.call-done = f32[64,128,128]{2,1,0:T(8,128)} async-done(((f32[8,128,128]{2,1,0:T(8,128)}), f32[64,128,128]{2,1,0:T(8,128)}) %all-gather.8.cloned.1.call-update) | async-done | bytes 4194320 | tf_op jit(solution)/shard_map/all_gather | solution.py:18
  226.8 8.8 %while.82 = (s32[]{:T(128)}, f32[8,128,128]{2,1,0:T(8,128)S(1)}, s32[]{:T(128)}, f32[8,8]{1,0:T(8,128)S(1)}, f32[8,8,128,128]{3,2,1,0:T(8,128)}, /*index=5*/s32[]{:T(128)}, s32[]{:T(128)}, s32[]{:T(128)}, s32[]{:T(128)}) while((s32[]{:T(128)}, f32[8,128,128]{2,1,0:T(8,128)S(1)}, s32[]{:T(128)}, f32[8,8]{1,0:T(8,128)S(1)}, ...), condition=%wide.region_15.16_spmd, body=%wide.region_14.15_spmd.sunk | while | flops 262150 | bytes 1573107 | solution.py:27
  226.9 1.2 bitcast_add_fusion.9
  228.1 1.2 bitcast_add_fusion.9
  229.3 1.2 bitcast_add_fusion.9
  230.6 1.2 bitcast_add_fusion.9
  231.8 1.2 bitcast_add_fusion.9
  233.0 1.2 bitcast_add_fusion.9
  234.3 1.2 bitcast_add_fusion.9
  235.7 2.3 multiply_add_fusion
  238.0 31.1 %while.83 = (s32[]{:T(128)}, bf16[2,256,8,128]{1,3,2,0:T(8,128)(2,1)}, bf16[2,256,8,128]{1,3,2,0:T(8,128)(2,1)}, bf16[2,256,8,128]{1,3,2,0:T(8,128)(2,1)}, bf16[...) while((s32[]{:T(128)}, ...), condition=%wide.region_17.18_spmd, body=%wide.region_16.17_spmd.sunk | while | flops 1886717952 | bytes 60595176 | solution.py:152
  238.4 1.0 copy-done
  239.4 1.7 multiply_convert_fusion.4
  241.1 1.4 convolution_bitcast_fusion.9
  242.8 2.8 fusion.151
  246.0 2.4 fusion.150
  248.4 1.6 fusion.152
  250.1 3.5 %fusion.153 = bf16[2,256,8,128]{1,3,2,0:T(8,128)(2,1)} fusion(bf16[2,256,8,128]{1,3,2,0:T(8,128)(2,1)} %get-tuple-element.961, s32[]{:T(128)} %get-tuple-element.958, f32[256,8,128]{0,2,1:T(8,128)} %fusion.152, f32[8,256]{1,0:T(8,128)S(1)} %dynamic-slice_bitcast_fusion.5, pred[256,256]{1,0:T(8,128)(4,1)S(1)} %iota_compare_fusion.5, ...), kind=kOutput, calls=%fused_computation.64.clone.1 | convolution fusion | flops 271581184 | bytes 3229184 | tf_op jit(solution)/shard_map/while/body/eval_jaxpr/hts,the->she/dot_general | solution.py:138
  254.9 1.7 multiply_convert_fusion.4
  256.6 1.4 convolution_bitcast_fusion.9
  258.4 2.8 fusion.151
  261.6 2.4 fusion.150
  264.0 1.6 fusion.152
  265.6 3.5 %fusion.153 = bf16[2,256,8,128]{1,3,2,0:T(8,128)(2,1)} fusion(bf16[2,256,8,128]{1,3,2,0:T(8,128)(2,1)} %get-tuple-element.961, s32[]{:T(128)} %get-tuple-element.958, f32[256,8,128]{0,2,1:T(8,128)} %fusion.152, f32[8,256]{1,0:T(8,128)S(1)} %dynamic-slice_bitcast_fusion.5, pred[256,256]{1,0:T(8,128)(4,1)S(1)} %iota_compare_fusion.5, ...), kind=kOutput, calls=%fused_computation.64.clone.1 | convolution fusion | flops 271581184 | bytes 3229184 | tf_op jit(solution)/shard_map/while/body/eval_jaxpr/hts,the->she/dot_general | solution.py:138
  269.1 1.5 copy.118
  270.6 4.6 %all_to_all.152 = bf16[2,256,1024]{2,1,0:T(8,128)(2,1)S(1)} all-to-all(bf16[2,256,1024]{2,1,0:T(8,128)(2,1)S(1)} %copy.118), channel_id=1, replica_groups=mesh['parts'=2,'seq'=8,'head'=2] {'head'}, dimensions={0} | all-to-all | bytes 2097152 | tf_op jit(solution)/shard_map/all_to_all | solution.py:161
  275.7 1.4 copy.106
  277.7 4.6 %all_to_all.153 = bf16[2,256,1024]{2,1,0:T(8,128)(2,1)S(1)} all-to-all(bf16[2,256,1024]{2,1,0:T(8,128)(2,1)S(1)} %copy.119), channel_id=1, replica_groups=mesh['parts'=2,'seq'=8,'head'=2] {'head'}, dimensions={0} | all-to-all | bytes 2097152 | tf_op jit(solution)/shard_map/all_to_all | solution.py:162
  282.8 1.4 copy.107
  284.7 4.6 %all_to_all.154 = bf16[2,256,1024]{2,1,0:T(8,128)(2,1)S(1)} all-to-all(bf16[2,256,1024]{2,1,0:T(8,128)(2,1)S(1)} %copy.120), channel_id=1, replica_groups=mesh['parts'=2,'seq'=8,'head'=2] {'head'}, dimensions={0} | all-to-all | bytes 2097152 | tf_op jit(solution)/shard_map/all_to_all | solution.py:163
  289.8 1.4 copy.108
  (127 shorter events, 12.8 us)
Async XLA Ops:
  7.2 5.6 %all-to-all-start.3 = ((bf16[256,2,8]{0,2,1:T(8,128)(2,1)}), bf16[256,2,8]{0,2,1:T(8,128)(2,1)S(1)}, u32[]{:S(2)}, u32[]{:S(2)}) async-start(bf16[256,2,8]{0,2,1:T(8,128)(2,1)} %bitcast.318), calls=%async_computation.3 | async-start | bytes 16384 | tf_op jit(solution)/shard_map/all_to_all | solution.py:48
  10.4 7.7 %copy-start.12 = (bf16[256,2048]{1,0:T(8,128)(2,1)S(1)}, bf16[256,2048]{1,0:T(8,128)(2,1)}, u32[]{:S(2)}) copy-start(bf16[256,2048]{1,0:T(8,128)(2,1)} %param.18) | copy-start | bytes 3145732
  12.8 6.7 %all-to-all-start = ((bf16[256,2,1024]{0,2,1:T(8,128)(2,1)}), bf16[256,2,1024]{0,2,1:T(8,128)(2,1)S(1)}, u32[]{:S(2)}, u32[]{:S(2)}) async-start(bf16[256,2,1024]{0,2,1:T(8,128)(2,1)} %bitcast.32), calls=%async_computation | async-start | bytes 2097152 | tf_op jit(solution)/shard_map/all_to_all | solution.py:46
  16.4 93.5 %all-gather.6.cloned.1.call-start = ((), (), s32[]{:S(2)}) async-start(), calls=%async_computation.9 | async-start | bytes 4718592 | tf_op jit(solution)/shard_map/all_gather | solution.py:18
  19.5 7.8 %copy-start.9 = (bf16[256,2,1024]{0,2,1:T(8,128)(2,1)}, bf16[256,2,1024]{0,2,1:T(8,128)(2,1)S(1)}, u32[]{:S(2)}) copy-start(bf16[256,2,1024]{0,2,1:T(8,128)(2,1)S(1)} %all-to-all-done) | copy-start | bytes 3145732
  28.4 4.9 %copy-start.13 = (bf16[256,2048]{1,0:T(8,128)(2,1)S(1)}, bf16[256,2048]{1,0:T(8,128)(2,1)}, u32[]{:S(2)}) copy-start(bf16[256,2048]{1,0:T(8,128)(2,1)} %param.17) | copy-start | bytes 3145732
  32.4 0.8 copy-start.3
  33.3 5.9 %copy-start.19 = (u32[32]{0:T(128)S(1)}, u32[32]{0:T(128)}, u32[]{:S(2)}) copy-start(u32[32]{0:T(128)} %constant.163) | copy-start | bytes 388
  34.6 29.8 %copy-start.14 = (bf16[256,2048]{1,0:T(8,128)(2,1)S(1)}, bf16[256,2048]{1,0:T(8,128)(2,1)}, u32[]{:S(2)}) copy-start(bf16[256,2048]{1,0:T(8,128)(2,1)} %param.20) | copy-start | bytes 3145732
  34.6 76.7 %all-to-all-start.1 = ((bf16[256,2,1024]{0,2,1:T(8,128)(2,1)}), bf16[256,2,1024]{0,2,1:T(8,128)(2,1)}, u32[]{:S(2)}, u32[]{:S(2)}) async-start(bf16[256,2,1024]{0,2,1:T(8,128)(2,1)} %bitcast.35), calls=%async_computation.1 | async-start | bytes 2097152 | tf_op jit(solution)/shard_map/all_to_all | solution.py:44
  111.3 19.4 %all-to-all-start.5 = ((bf16[256,2,1024]{0,2,1:T(8,128)(2,1)}), bf16[256,2,1024]{0,2,1:T(8,128)(2,1)}, u32[]{:S(2)}, u32[]{:S(2)}) async-start(bf16[256,2,1024]{0,2,1:T(8,128)(2,1)} %bitcast.306), calls=%async_computation.5 | async-start | bytes 2097152 | tf_op jit(solution)/shard_map/all_to_all | solution.py:47
  115.7 111.0 %all-gather.8.cloned.1.call-start = ((), (), s32[]{:S(2)}) async-start(), calls=%async_computation.10 | async-start | bytes 4718592 | tf_op jit(solution)/shard_map/all_gather | solution.py:18
  128.2 4.9 %copy-start.4 = (bf16[2,256,8,128]{1,3,2,0:T(8,128)(2,1)}, bf16[2,256,8,128]{1,3,2,0:T(8,128)(2,1)S(1)}, u32[]{:S(2)}) copy-start(bf16[2,256,8,128]{1,3,2,0:T(8,128)(2,1)S(1)} %get-tuple-element.992) | copy-start | bytes 3145732
  128.2 5.0 %copy-start.6 = (f32[2,8,128,128]{3,2,1,0:T(8,128)}, f32[2,8,128,128]{3,2,1,0:T(8,128)S(1)}, u32[]{:S(2)}) copy-start(f32[2,8,128,128]{3,2,1,0:T(8,128)S(1)} %get-tuple-element.993) | copy-start | bytes 3145732
  130.7 2.5 copy-start.10
  145.5 0.8 copy-start.2
  238.0 1.3 copy-start
  238.3 2.7 copy-start.11
  241.1 4.5 %copy-start.5 = (bf16[2,256,8,128]{1,3,2,0:T(8,128)(2,1)S(1)}, bf16[2,256,8,128]{1,3,2,0:T(8,128)(2,1)}, u32[]{:S(2)}) copy-start(bf16[2,256,8,128]{1,3,2,0:T(8,128)(2,1)} %get-tuple-element.976) | copy-start | bytes 3145732 | tf_op jit(solution)/shard_map/while
  242.8 3.2 %copy-start.7 = (f32[2,8,128,128]{3,2,1,0:T(8,128)S(1)}, f32[2,8,128,128]{3,2,1,0:T(8,128)}, u32[]{:S(2)}) copy-start(f32[2,8,128,128]{3,2,1,0:T(8,128)} %get-tuple-element.980) | copy-start | bytes 3145732 | tf_op jit(solution)/shard_map/while
  242.8 3.3 %copy-start.15 = (bf16[2,256,8,128]{1,3,2,0:T(8,128)(2,1)S(1)}, bf16[2,256,8,128]{1,3,2,0:T(8,128)(2,1)}, u32[]{:S(2)}) copy-start(bf16[2,256,8,128]{1,3,2,0:T(8,128)(2,1)} %get-tuple-element.959) | copy-start | bytes 3145732 | tf_op jit(solution)/shard_map/while
  246.0 2.4 copy-start.8
  248.4 1.6 copy-start.16
  250.1 3.5 %copy-start.1 = (f32[2,256,8,128]{1,3,2,0:T(8,128)S(1)}, f32[2,256,8,128]{1,3,2,0:T(8,128)}, u32[]{:S(2)}) copy-start(f32[2,256,8,128]{1,3,2,0:T(8,128)} %copy-done) | copy-start | bytes 6291460 | tf_op jit(solution)/shard_map/while
  253.6 1.3 copy-start
  253.9 2.7 copy-start.11
  256.6 4.5 %copy-start.5 = (bf16[2,256,8,128]{1,3,2,0:T(8,128)(2,1)S(1)}, bf16[2,256,8,128]{1,3,2,0:T(8,128)(2,1)}, u32[]{:S(2)}) copy-start(bf16[2,256,8,128]{1,3,2,0:T(8,128)(2,1)} %get-tuple-element.976) | copy-start | bytes 3145732 | tf_op jit(solution)/shard_map/while
  258.3 3.3 %copy-start.7 = (f32[2,8,128,128]{3,2,1,0:T(8,128)S(1)}, f32[2,8,128,128]{3,2,1,0:T(8,128)}, u32[]{:S(2)}) copy-start(f32[2,8,128,128]{3,2,1,0:T(8,128)} %get-tuple-element.980) | copy-start | bytes 3145732 | tf_op jit(solution)/shard_map/while
  258.3 3.3 %copy-start.15 = (bf16[2,256,8,128]{1,3,2,0:T(8,128)(2,1)S(1)}, bf16[2,256,8,128]{1,3,2,0:T(8,128)(2,1)}, u32[]{:S(2)}) copy-start(bf16[2,256,8,128]{1,3,2,0:T(8,128)(2,1)} %get-tuple-element.959) | copy-start | bytes 3145732 | tf_op jit(solution)/shard_map/while
  261.6 2.4 copy-start.8
  264.0 1.6 copy-start.16
  265.6 3.5 %copy-start.1 = (f32[2,256,8,128]{1,3,2,0:T(8,128)S(1)}, f32[2,256,8,128]{1,3,2,0:T(8,128)}, u32[]{:S(2)}) copy-start(f32[2,256,8,128]{1,3,2,0:T(8,128)} %copy-done) | copy-start | bytes 6291460 | tf_op jit(solution)/shard_map/while
  275.2 2.0 copy-start.17
  282.2 2.0 copy-start.18
Sparse Core Ops, SparseCore 0:
  33.4 76.4 all-gather.5
  146.4 80.3 all-gather.7
where the time goes:
time: 300 us; the launch traced here: 298 us
  waiting for transfers between devices  118 us (39%)
  blocking collectives  48.7 us (16%)
  matrix products  46.4 us (15%)
  other arithmetic  29.5 us (10%)
  local copies, waits for them, and re-layouts  24.3 us (8%)
  starting transfers between devices  15.9 us (5%)
  between operations  15 us (5%)
    all_gather x2, waiting for transfers between devices, entering(): gathered = jax.tree.map(lambda a: lax.all_gather(a, axis), part)  117 us
    unnamed x1, blocking collectives  23.6 us
    unnamed x33, local copies, waits for them, and re-layouts  11.9 us
    add x7, other arithmetic, combine_states(): jnp.exp(later[0])[:, None, None] * earlier[1] + later[1]  8.33 us
    dot_general x2, matrix products, backward_block(): jnp.einsum('hts,the->she', scores.astype(jnp.bfloat16), grad_short, prefe...  6.99 us
    dot_general x2, matrix products, forward_block(): jnp.einsum('hts,she->the', scores.astype(jnp.bfloat16), value_b, preferre...  6.97 us
  transfers between devices with their start and end apart: 6, of which 2 were waited for; matrix products, arithmetic and copies ran while one was open for 9% of the time, Pallas kernels for 0%

commit v1 on v0

v1 whole, which is shorter than its diff:
```python
import functools

import jax
import jax.numpy as jnp
from jax import lax
from jax.experimental import pallas as pl
from jax.experimental.pallas import tpu as pltpu
from jax.sharding import PartitionSpec as P

DH = 128
EPSILON = 1e-06
CHUNKS = 4
F32 = jnp.float32
BF16 = jnp.bfloat16
MESH = pl.DeviceIdType.MESH


def dot(a, b, contract):
    return lax.dot_general(a, b, ((contract[0], contract[1]), ((), ())), preferred_element_type=F32)


NN = ((1,), (0,))
NT = ((1,), (1,))
TN = ((0,), (0,))


def kernel(
    groups, heads, q_hbm, k_hbm, v_hbm, g_hbm, ld_ref, o_hbm, dq_hbm, dk_hbm, dv_hbm,
    q, k, v, g, o, dq, dk, dv, colb, wrow, bias, wgt, sb, intra, gs, kpart,
    st, cc, tt, m1s, m1r, m2s, m2r, m3s, m3r, m4s, ent,
    in_sem, out_sem, ss, rs, ts, tr,
):
    rows = q.shape[0]
    half = heads // 2
    per = half // CHUNKS
    wire = m1s.dtype
    seq = lax.axis_index("seq")
    c = lax.axis_index("head")
    group = seq // 2
    y = seq - 2 * group
    twin = 2 * group + (1 - y)
    partner = {"head": 1 - c}
    peers = (partner, {"seq": twin}, {"seq": twin, "head": 1 - c})
    has_before = group > 0
    has_after = group < groups - 1

    loads = [
        pltpu.make_async_copy(a, b, in_sem.at[i])
        for i, (a, b) in enumerate(((k_hbm, k), (v_hbm, v), (q_hbm, q), (g_hbm, g)))
    ]
    for load in loads:
        load.start()

    barrier = pltpu.get_barrier_semaphore()
    for peer in peers:
        pl.semaphore_signal(barrier, inc=1, device_id=peer, device_id_type=MESH)

    @pl.when(has_before)
    def _():
        pl.semaphore_signal(barrier, inc=1, device_id={"seq": seq - 2}, device_id_type=MESH)

    @pl.when(has_after)
    def _():
        pl.semaphore_signal(barrier, inc=1, device_id={"seq": seq + 2}, device_id_type=MESH)

    def cols(h):
        return pl.ds(pl.multiple_of(h * DH, DH), DH)

    row_i = lax.broadcasted_iota(jnp.int32, (rows, rows), 0)
    col_i = lax.broadcasted_iota(jnp.int32, (rows, rows), 1)
    lower = row_i >= col_i
    bias[...] = jnp.where(lower, 0.0, -1e30)
    tri = jnp.where(lower, 1.0, 0.0).astype(BF16)
    ld = ld_ref[...]
    within = dot(tri, ld, NN)
    wrow[...] = dot(ld, tri, ((0,), (1,)))
    for h in range(heads):
        spread = jnp.broadcast_to(within[:, h : h + 1], (rows, DH))
        colb[h] = spread
        tt[0, h : h + 1, :] = spread[rows - 1 : rows, :]

    pl.semaphore_wait(barrier, 3 + has_before.astype(jnp.int32) + has_after.astype(jnp.int32))

    def total_copy(i):
        return pltpu.make_async_remote_copy(
            src_ref=tt.at[0], dst_ref=tt.at[i + 1], send_sem=ts.at[i], recv_sem=tr.at[i],
            device_id=peers[i], device_id_type=MESH,
        )

    for i in range(3):
        total_copy(i).start()

    def remote(kind, d, ch, src, dst, peer):
        return pltpu.make_async_remote_copy(
            src_ref=src, dst_ref=dst, send_sem=ss.at[kind, d, ch], recv_sem=rs.at[kind, d, ch],
            device_id=peer, device_id_type=MESH,
        )

    def move1(d, ch):
        part = pl.ds(ch * per, per)
        return remote(0, d, ch, m1s.at[d, part], m1r.at[d, part], partner)

    def move2(d, ch):
        part = pl.ds(ch * per, per)
        return remote(1, d, ch, m2s.at[d, part], m2r.at[d, part], {"seq": twin})

    def move3(d, ch):
        part = pl.ds(ch * per, per)
        step = 2 if d == 0 else -2
        return remote(2, d, ch, m3s.at[d, part], m3r.at[d, part], {"seq": seq + step})

    def move4(d, ch, base):
        part = pl.ds(ch * per, per)
        return remote(3, d, ch, m4s.at[d, part], ent.at[d, pl.ds(base * half + ch * per, per)], partner)

    def chunked(body):
        lax.fori_loop(0, CHUNKS, lambda ch, _: (body(ch), 0)[1], 0)

    def each(count, body):
        lax.fori_loop(0, count, lambda i, _: (body(i), 0)[1], 0)

    def total(rel, h):
        return tt[rel, pl.ds(h, 1), :]

    def combine_cores(d, ch):
        move1(d, ch).wait_recv()
        first = (c if d == 0 else 1 - c) == 0
        for i in range(per):
            j = ch * per + i
            h = c * half + j
            mine, other = st[d, j], m1r[d, j].astype(F32)
            fade_mine = jnp.where(first, jnp.exp(total(1, h)), 1.0)
            fade_other = jnp.where(first, 1.0, jnp.exp(total(0, h)))
            both = fade_mine * mine + fade_other * other
            cc[j] = both
            m2s[d, j] = both.astype(wire)
        move2(d, ch).start()

    def chain(d, ch):
        has_in = has_before if d == 0 else has_after
        has_out = has_after if d == 0 else has_before
        first = (c if d == 0 else 1 - c) == 0
        first_chip = (y if d == 0 else 1 - y) == 0
        move2(d, ch).wait_recv()

        @pl.when(has_in)
        def _():
            move3(d, ch).wait_recv()

        @pl.when(has_out)
        def _():
            for i in range(per):
                j = ch * per + i
                h = c * half + j
                t_mine = total(0, h) + total(1, h)
                t_other = total(2, h) + total(3, h)
                fade_mine = jnp.where(first_chip, jnp.exp(t_other), 1.0)
                fade_other = jnp.where(first_chip, 1.0, jnp.exp(t_mine))
                whole = fade_mine * cc[j] + fade_other * m2r[d, j].astype(F32)
                m3s[d, j] = (jnp.exp(t_mine + t_other) * m3r[d, j].astype(F32) + whole).astype(wire)
            move3(d, ch).start()

        for i in range(per):
            j = ch * per + i
            h = c * half + j
            t_other = total(2, h) + total(3, h)
            fade_in = jnp.where(first_chip, 1.0, jnp.exp(t_other))
            add_in = jnp.where(first_chip, 0.0, 1.0)
            chip_in = fade_in * m3r[d, j].astype(F32) + add_in * m2r[d, j].astype(F32)
            t_first = jnp.where(first, total(0, h), total(1, h))
            state_first = jnp.where(first, st[d, j], m1r[d, j].astype(F32))
            later = jnp.exp(t_first) * chip_in + state_first
            ent[d, h] = jnp.where(first, chip_in, later).astype(wire)
            m4s[d, j] = jnp.where(first, later, chip_in).astype(wire)
        move4(d, ch, c).start()

    @pl.when(jnp.logical_not(has_before))
    def _():
        m3r[0] = jnp.zeros(m3r.shape[1:], wire)

    @pl.when(jnp.logical_not(has_after))
    def _():
        m3r[1] = jnp.zeros(m3r.shape[1:], wire)

    loads[0].wait()
    loads[1].wait()

    def local_state(h):
        fading = jnp.exp(total(0, h) - colb[h])
        faded = (k[:, cols(h)].astype(F32) * fading).astype(BF16)
        return dot(faded, v[:, cols(h)], TN)

    def send_local(ch):
        for i in range(per):
            j = ch * per + i
            m1s[0, j] = local_state((1 - c) * half + j).astype(wire)
        move1(0, ch).start()

    chunked(send_local)

    def keep_local(ch):
        for i in range(per):
            j = ch * per + i
            st[0, j] = local_state(c * half + j)

    chunked(keep_local)
    loads[2].wait()

    def inside(h):
        column = colb[h]
        spread = jnp.concatenate([column, column], axis=1) - wrow[pl.ds(h, 1), :]
        weights = jnp.exp(jnp.minimum(spread, bias[...]))
        wgt[h] = weights
        scores = (dot(q[:, cols(h)], k[:, cols(h)], NT) * weights).astype(BF16)
        sb[h] = scores
        intra[h] = dot(scores, v[:, cols(h)], NN)

    def inside_own(i):
        inside(c * half + 2 * i)
        inside(c * half + 2 * i + 1)

    def inside_partner(i):
        inside((1 - c) * half + 2 * i)
        inside((1 - c) * half + 2 * i + 1)

    each(half // 4, inside_own)
    for i in range(3):
        total_copy(i).wait_recv()
    chunked(lambda ch: combine_cores(0, ch))
    lax.fori_loop(half // 4, half // 2, lambda i, _: (inside_own(i), 0)[1], 0)
    chunked(lambda ch: chain(0, ch))
    each(half // 2, inside_partner)
    loads[3].wait()

    def normalize(h):
        growing = jnp.exp(colb[h])
        q_h = q[:, cols(h)]
        numer = intra[h] + growing * dot(q_h, ent[0, h].astype(BF16), NN)
        inv = lax.rsqrt(jnp.mean(numer * numer, axis=-1, keepdims=True) + EPSILON)
        normed = numer * inv
        o[:, cols(h)] = normed.astype(BF16)
        g_h = g[:, cols(h)].astype(F32)
        grad = (g_h - normed * jnp.mean(g_h * normed, axis=-1, keepdims=True)) * inv
        short = grad.astype(BF16)
        gs[h] = short
        grown = (q_h.astype(F32) * growing).astype(BF16)
        return dot(grown, short, TN)

    def normalize_own(ch):
        for i in range(per):
            j = ch * per + i
            st[1, j] = normalize(c * half + j)

    def normalize_partner(ch):
        move4(0, ch, 1 - c).wait_recv()
        for i in range(per):
            j = ch * per + i
            m1s[1, j] = normalize((1 - c) * half + j).astype(wire)
        move1(1, ch).start()

    chunked(normalize_own)
    chunked(normalize_partner)
    out_copies = [
        pltpu.make_async_copy(a, b, out_sem.at[i])
        for i, (a, b) in enumerate(((o, o_hbm), (dq, dq_hbm), (dk, dk_hbm), (dv, dv_hbm)))
    ]
    out_copies[0].start()

    def gradients(h):
        short = gs[h]
        k_h = k[:, cols(h)]
        mixed = (dot(short, v[:, cols(h)], NT) * wgt[h]).astype(BF16)
        cross = dot(short, ent[0, h].astype(BF16), NT)
        dq[:, cols(h)] = (dot(mixed, k_h, NN) + jnp.exp(colb[h]) * cross).astype(BF16)
        kpart[h] = dot(mixed, q[:, cols(h)], TN)
        intra[h] = dot(sb[h], short, TN)

    def gradients_own(i):
        gradients(c * half + 2 * i)
        gradients(c * half + 2 * i + 1)

    def gradients_partner(i):
        gradients((1 - c) * half + 2 * i)
        gradients((1 - c) * half + 2 * i + 1)

    each(half // 4, gradients_own)
    chunked(lambda ch: combine_cores(1, ch))
    lax.fori_loop(half // 4, half // 2, lambda i, _: (gradients_own(i), 0)[1], 0)
    chunked(lambda ch: chain(1, ch))
    each(half // 2, gradients_partner)
    out_copies[1].start()

    def finish(h):
        fading = jnp.exp(total(0, h) - colb[h])
        back = ent[1, h].astype(BF16)
        dk[:, cols(h)] = (kpart[h] + fading * dot(v[:, cols(h)], back, NT)).astype(BF16)
        dv[:, cols(h)] = (intra[h] + fading * dot(k[:, cols(h)], back, NN)).astype(BF16)

    def finish_own(ch):
        for i in range(per):
            finish(c * half + ch * per + i)

    def finish_partner(ch):
        move4(1, ch, 1 - c).wait_recv()
        for i in range(per):
            finish((1 - c) * half + ch * per + i)

    chunked(finish_own)
    chunked(finish_partner)
    out_copies[2].start()
    out_copies[3].start()

    for i in range(3):
        total_copy(i).wait_send()
    for d in range(2):

        def drain(ch, d=d):
            move1(d, ch).wait_send()
            move2(d, ch).wait_send()
            move4(d, ch, c).wait_send()

            @pl.when(has_after if d == 0 else has_before)
            def _():
                move3(d, ch).wait_send()

        chunked(drain)
    for copy in out_copies:
        copy.wait()


def body(groups, queries, keys, values, out_grad, log_decay):
    rows, width = queries.shape
    heads = width // DH
    half = heads // 2
    wire = BF16 if groups <= 8 else F32
    array = jax.ShapeDtypeStruct((rows, width), BF16)
    any_spec = pl.BlockSpec(memory_space=pl.ANY)
    moved = pltpu.VMEM((2, half, DH, DH), wire)
    return pl.pallas_call(
        functools.partial(kernel, groups, heads),
        out_shape=(array,) * 4,
        in_specs=[any_spec] * 4 + [pl.BlockSpec(memory_space=pltpu.VMEM)],
        out_specs=(any_spec,) * 4,
        scratch_shapes=[pltpu.VMEM((rows, width), BF16)] * 8
        + [
            pltpu.VMEM((heads, rows, DH), F32),
            pltpu.VMEM((heads, rows), F32),
            pltpu.VMEM((rows, rows), F32),
            pltpu.VMEM((heads, rows, rows), F32),
            pltpu.VMEM((heads, rows, rows), BF16),
            pltpu.VMEM((heads, rows, DH), F32),
            pltpu.VMEM((heads, rows, DH), BF16),
            pltpu.VMEM((heads, rows, DH), F32),
            pltpu.VMEM((2, half, DH, DH), F32),
            pltpu.VMEM((half, DH, DH), F32),
            pltpu.VMEM((4, heads, DH), F32),
        ]
        + [moved] * 7
        + [
            pltpu.VMEM((2, heads, DH, DH), wire),
            pltpu.SemaphoreType.DMA((4,)),
            pltpu.SemaphoreType.DMA((4,)),
            pltpu.SemaphoreType.DMA((4, 2, CHUNKS)),
            pltpu.SemaphoreType.DMA((4, 2, CHUNKS)),
            pltpu.SemaphoreType.DMA((3,)),
            pltpu.SemaphoreType.DMA((3,)),
        ],
        compiler_params=pltpu.CompilerParams(
            collective_id=0, has_side_effects=True, vmem_limit_bytes=52 * 1024 * 1024
        ),
    )(queries, keys, values, out_grad, log_decay)


def solution(mesh):
    placed = P(("parts", "seq", "head"), None)
    return jax.shard_map(
        functools.partial(body, mesh.shape["seq"] // 2),
        mesh=mesh,
        in_specs=(placed,) * 5,
        out_specs=(placed,) * 4,
        check_vma=False,
    )
```

time: 300 us -> 62.5 us (0.21)
  waiting for transfers between devices: 118 us -> 0 us
  Pallas kernels: 0 us -> 55 us
  blocking collectives: 48.7 us -> 0 us
  matrix products: 46.4 us -> 0 us
  other arithmetic: 29.5 us -> 0 us
  local copies, waits for them, and re-layouts: 24.3 us -> 6.59 us
  starting transfers between devices: 15.9 us -> 0 us
  between operations: 15 us -> 0.65 us
    all_gather x2 -> x0, waiting for transfers between devices: 117 us -> none  [entering(): gathered = jax.tree.map(lambda a: lax.all_gather(a, axis), part)]
    pallas_call x0 -> x1, Pallas kernels: none -> 55 us  [body(): pl.pallas_call(functools.partial(kernel, groups, heads), out_shape=(array...]
    dot_general x20 -> x0, matrix products: 46.4 us -> none  [the longest x2 6.99 us: backward_block(): jnp.einsum('hts,the->she', scores.astype(jnp.bfloat16), grad_short, prefe...]
    all_to_all x5 -> x0, blocking collectives: 25.1 us -> none  [the longest x1 5.69 us: body(): lax.all_to_all(out_rows, 'head', split_axis=0, concat_axis=1, tiled=True)]
    unnamed x1 -> x0, blocking collectives: 23.6 us -> none
    add x13 -> x0, other arithmetic: 16.7 us -> none  [the longest x7 8.33 us: combine_states(): jnp.exp(later[0])[:, None, None] * earlier[1] + later[1]]
    all_to_all x4 -> x0, starting transfers between devices: 15.8 us -> none  [the longest x1 4.55 us: body(): lax.all_to_all(queries, 'head', split_axis=1, concat_axis=0, tiled=True)]
    all_to_all x8 -> x0, local copies, waits for them, and re-layouts: 6.7 us -> none  [the longest x2 2 us: body(): lax.all_to_all(query_flat, 'head', split_axis=0, concat_axis=1, tiled=True)]
  transfers between devices with their start and end apart: 6 -> 0, of which waited for: 2 -> 0; matrix products, arithmetic and copies ran while one was open for 9% -> 0% of each run, Pallas kernels for 0% -> 0%
where the time goes in v1:
time: 62.5 us; the launch traced here: 62.2 us
  Pallas kernels  55 us (88%)
  local copies, waits for them, and re-layouts  6.59 us (11%)
  between operations  0.65 us (1%)
    pallas_call x1, Pallas kernels, body(): pl.pallas_call(functools.partial(kernel, groups, heads), out_shape=(array...  55 us
    unnamed x11, local copies, waits for them, and re-layouts  6.59 us

profile of v1, /device:TPU:0, one launch (start us, length us, event | category | flops | bytes accessed | tf_op | source)
XLA Modules:
  0.0 62.2 jit_solution(12105326398691921696)
XLA Ops:
  0.6 0.8 %copy.9.ld_ref = bf16[256,16]{1,0:T(8,128)(2,1)S(1)} copy(bf16[256,16]{0,1:T(8,128)(2,1)} %param.9) | data formatting | bytes 16384 | tf_op args[4]
  1.4 55.0 %shard_map.84 = (bf16[256,2048]{1,0:T(8,128)(2,1)S(1)}, bf16[256,2048]{1,0:T(8,128)(2,1)}, bf16[256,2048]{1,0:T(8,128)(2,1)}, bf16[256,2048]{1,0:T(8,128)(2,1)}) custom-call(bf16[256,2048]{1,0:T(8,128)(2,1)} %q_hbm.1, bf16[256,2048]{1,0:T(8,128)(2,1)} %k_hbm.1, bf16[256,2048]{1,0:T(8,128)(2,1)} %v_hbm.1, bf16[256,2048]{1,0:T(8,128)(2,1)} %g_hbm.1, ...), custom_call_target="tpu_custom_call" | custom-call | tf_op jit(solution)/shard_map/pallas_call | solution.py:339
  56.5 0.0 copy-start.2
  56.5 1.0 %copy.14 = bf16[256,2048]{1,0:T(8,128)(2,1)} copy(bf16[256,2048]{1,0:T(8,128)(2,1)S(1)} %get-tuple-element.8) | data formatting | bytes 2097152
  57.4 0.6 copy-done.2
  58.1 0.0 copy-start.1
  58.1 1.0 %copy.15 = bf16[256,2048]{1,0:T(8,128)(2,1)} copy(bf16[256,2048]{1,0:T(8,128)(2,1)S(1)} %copy-done.2) | data formatting | bytes 2097152
  59.0 0.6 %copy-done.1 = bf16[256,2048]{1,0:T(8,128)(2,1)S(1)} copy-done((bf16[256,2048]{1,0:T(8,128)(2,1)S(1)}, bf16[256,2048]{1,0:T(8,128)(2,1)}, u32[]{:S(2)}) %copy-start.1) | copy-done | bytes 1048600
  59.7 0.0 copy-start
  59.7 1.0 %copy.16 = bf16[256,2048]{1,0:T(8,128)(2,1)} copy(bf16[256,2048]{1,0:T(8,128)(2,1)S(1)} %copy-done.1) | data formatting | bytes 2097152
  60.6 0.6 %copy-done = bf16[256,2048]{1,0:T(8,128)(2,1)S(1)} copy-done((bf16[256,2048]{1,0:T(8,128)(2,1)S(1)}, bf16[256,2048]{1,0:T(8,128)(2,1)}, u32[]{:S(2)}) %copy-start) | copy-done | bytes 1048600
  61.3 1.0 %copy.17 = bf16[256,2048]{1,0:T(8,128)(2,1)} copy(bf16[256,2048]{1,0:T(8,128)(2,1)S(1)} %copy-done) | data formatting | bytes 2097152
Async XLA Ops:
  56.5 1.6 %copy-start.2 = (bf16[256,2048]{1,0:T(8,128)(2,1)S(1)}, bf16[256,2048]{1,0:T(8,128)(2,1)}, u32[]{:S(2)}) copy-start(bf16[256,2048]{1,0:T(8,128)(2,1)} %get-tuple-element.9) | copy-start | bytes 3145732
  58.1 1.6 %copy-start.1 = (bf16[256,2048]{1,0:T(8,128)(2,1)S(1)}, bf16[256,2048]{1,0:T(8,128)(2,1)}, u32[]{:S(2)}) copy-start(bf16[256,2048]{1,0:T(8,128)(2,1)} %get-tuple-element.10) | copy-start | bytes 3145732
  59.7 1.6 %copy-start = (bf16[256,2048]{1,0:T(8,128)(2,1)S(1)}, bf16[256,2048]{1,0:T(8,128)(2,1)}, u32[]{:S(2)}) copy-start(bf16[256,2048]{1,0:T(8,128)(2,1)} %get-tuple-element.11) | copy-start | bytes 3145732

commit v2 on v1

--- a/solution.py
+++ b/solution.py
@@ -19,16 +19,23 @@
     return lax.dot_general(a, b, ((contract[0], contract[1]), ((), ())), preferred_element_type=F32)
 
 
+def lane_mean(a):
+    high = a.astype(BF16)
+    low = (a - high.astype(F32)).astype(BF16)
+    share = jnp.full((2 * DH, DH), 1.0 / DH, BF16)
+    return dot(jnp.concatenate([high, low], axis=1), share, NN)
+
+
 NN = ((1,), (0,))
 NT = ((1,), (1,))
 TN = ((0,), (0,))
 
 
 def kernel(
-    groups, heads, q_hbm, k_hbm, v_hbm, g_hbm, ld_ref, o_hbm, dq_hbm, dk_hbm, dv_hbm,
-    q, k, v, g, o, dq, dk, dv, colb, wrow, bias, wgt, sb, intra, gs, kpart,
+    groups, heads, q_hbm, k_hbm, v_hbm, g_hbm, ld_hbm, o, dq, dk, dv,
+    q, k, v, g, ld_ref, colb, wrow, bias, wgt, sb, intra, gs, kpart,
     st, cc, tt, m1s, m1r, m2s, m2r, m3s, m3r, m4s, ent,
-    in_sem, out_sem, ss, rs, ts, tr,
+    in_sem, ss, rs, ts, tr,
 ):
     rows = q.shape[0]
     half = heads // 2
@@ -46,10 +53,12 @@
 
     loads = [
         pltpu.make_async_copy(a, b, in_sem.at[i])
-        for i, (a, b) in enumerate(((k_hbm, k), (v_hbm, v), (q_hbm, q), (g_hbm, g)))
+        for i, (a, b) in enumerate(
+            ((k_hbm, k), (v_hbm, v), (q_hbm, q), (g_hbm, g), (ld_hbm, ld_ref))
+        )
     ]
-    for load in loads:
-        load.start()
+    for i in (4, 0, 1, 2, 3):
+        loads[i].start()
 
     barrier = pltpu.get_barrier_semaphore()
     for peer in peers:
@@ -71,6 +80,7 @@
     lower = row_i >= col_i
     bias[...] = jnp.where(lower, 0.0, -1e30)
     tri = jnp.where(lower, 1.0, 0.0).astype(BF16)
+    loads[4].wait()
     ld = ld_ref[...]
     within = dot(tri, ld, NN)
     wrow[...] = dot(ld, tri, ((0,), (1,)))
@@ -104,10 +114,10 @@
         part = pl.ds(ch * per, per)
         return remote(1, d, ch, m2s.at[d, part], m2r.at[d, part], {"seq": twin})
 
-    def move3(d, ch):
-        part = pl.ds(ch * per, per)
+    def move3(d, j):
+        part = pl.ds(j, 1)
         step = 2 if d == 0 else -2
-        return remote(2, d, ch, m3s.at[d, part], m3r.at[d, part], {"seq": seq + step})
+        return remote(2, d, j, m3s.at[d, part], m3r.at[d, part], {"seq": seq + step})
 
     def move4(d, ch, base):
         part = pl.ds(ch * per, per)
@@ -116,8 +126,8 @@
     def chunked(body):
         lax.fori_loop(0, CHUNKS, lambda ch, _: (body(ch), 0)[1], 0)
 
-    def each(count, body):
-        lax.fori_loop(0, count, lambda i, _: (body(i), 0)[1], 0)
+    def span(start, stop, body):
+        lax.fori_loop(start, stop, lambda i, _: (body(i), 0)[1], 0)
 
     def total(rel, h):
         return tt[rel, pl.ds(h, 1), :]
@@ -136,30 +146,33 @@
             m2s[d, j] = both.astype(wire)
         move2(d, ch).start()
 
-    def chain(d, ch):
+    def relay(d, ch):
         has_in = has_before if d == 0 else has_after
         has_out = has_after if d == 0 else has_before
+        first_chip = (y if d == 0 else 1 - y) == 0
+        move2(d, ch).wait_recv()
+        for i in range(per):
+            j = ch * per + i
+            h = c * half + j
+            t_mine = total(0, h) + total(1, h)
+            t_other = total(2, h) + total(3, h)
+            fade_mine = jnp.where(first_chip, jnp.exp(t_other), 1.0)
+            fade_other = jnp.where(first_chip, 1.0, jnp.exp(t_mine))
+            fade_all = jnp.exp(t_mine + t_other)
+            whole = fade_mine * cc[j] + fade_other * m2r[d, j].astype(F32)
+
+            @pl.when(has_in)
+            def _():
+                move3(d, j).wait_recv()
+
+            @pl.when(has_out)
+            def _():
+                m3s[d, j] = (fade_all * m3r[d, j].astype(F32) + whole).astype(wire)
+                move3(d, j).start()
+
+    def enter(d, ch):
         first = (c if d == 0 else 1 - c) == 0
         first_chip = (y if d == 0 else 1 - y) == 0
-        move2(d, ch).wait_recv()
-
-        @pl.when(has_in)
-        def _():
-            move3(d, ch).wait_recv()
-
-        @pl.when(has_out)
-        def _():
-            for i in range(per):
-                j = ch * per + i
-                h = c * half + j
-                t_mine = total(0, h) + total(1, h)
-                t_other = total(2, h) + total(3, h)
-                fade_mine = jnp.where(first_chip, jnp.exp(t_other), 1.0)
-                fade_other = jnp.where(first_chip, 1.0, jnp.exp(t_mine))
-                whole = fade_mine * cc[j] + fade_other * m2r[d, j].astype(F32)
-                m3s[d, j] = (jnp.exp(t_mine + t_other) * m3r[d, j].astype(F32) + whole).astype(wire)
-            move3(d, ch).start()
-
         for i in range(per):
             j = ch * per + i
             h = c * half + j
@@ -174,6 +187,18 @@
             m4s[d, j] = jnp.where(first, later, chip_in).astype(wire)
         move4(d, ch, c).start()
 
+    def relay_all(d, has_out):
+        @pl.when(has_out)
+        def _():
+            chunked(lambda ch: relay(d, ch))
+
+    def arrive(d, ch, has_out):
+        @pl.when(jnp.logical_not(has_out))
+        def _():
+            relay(d, ch)
+
+        enter(d, ch)
+
     @pl.when(jnp.logical_not(has_before))
     def _():
         m3r[0] = jnp.zeros(m3r.shape[1:], wire)
@@ -215,32 +240,30 @@
         sb[h] = scores
         intra[h] = dot(scores, v[:, cols(h)], NN)
 
-    def inside_own(i):
-        inside(c * half + 2 * i)
-        inside(c * half + 2 * i + 1)
-
-    def inside_partner(i):
-        inside((1 - c) * half + 2 * i)
-        inside((1 - c) * half + 2 * i + 1)
-
-    each(half // 4, inside_own)
+    def inside_pair(i):
+        inside(2 * i)
+        inside(2 * i + 1)
+
     for i in range(3):
         total_copy(i).wait_recv()
     chunked(lambda ch: combine_cores(0, ch))
-    lax.fori_loop(half // 4, half // 2, lambda i, _: (inside_own(i), 0)[1], 0)
-    chunked(lambda ch: chain(0, ch))
-    each(half // 2, inside_partner)
+    early = jnp.where(has_before, half, 2)
+    span(0, early, inside_pair)
+    relay_all(0, has_after)
+    span(early, half, inside_pair)
     loads[3].wait()
 
     def normalize(h):
         growing = jnp.exp(colb[h])
         q_h = q[:, cols(h)]
         numer = intra[h] + growing * dot(q_h, ent[0, h].astype(BF16), NN)
-        inv = lax.rsqrt(jnp.mean(numer * numer, axis=-1, keepdims=True) + EPSILON)
+        g_h = g[:, cols(h)].astype(F32)
+        square = lane_mean(numer * numer)
+        along = lane_mean(g_h * numer)
+        inv = lax.rsqrt(square + EPSILON)
         normed = numer * inv
         o[:, cols(h)] = normed.astype(BF16)
-        g_h = g[:, cols(h)].astype(F32)
-        grad = (g_h - normed * jnp.mean(g_h * normed, axis=-1, keepdims=True)) * inv
+        grad = (g_h - normed * (along * inv)) * inv
         short = grad.astype(BF16)
         gs[h] = short
         grown = (q_h.astype(F32) * growing).astype(BF16)
@@ -258,13 +281,24 @@
             m1s[1, j] = normalize((1 - c) * half + j).astype(wire)
         move1(1, ch).start()
 
-    chunked(normalize_own)
-    chunked(normalize_partner)
-    out_copies = [
-        pltpu.make_async_copy(a, b, out_sem.at[i])
-        for i, (a, b) in enumerate(((o, o_hbm), (dq, dq_hbm), (dk, dk_hbm), (dv, dv_hbm)))
-    ]
-    out_copies[0].start()
+    def forward_step(ch):
+        arrive(0, ch, has_after)
+        normalize_own(ch)
+
+    def forward_both(ch):
+        forward_step(ch)
+        normalize_partner(ch - 1)
+
+        @pl.when(ch >= 2)
+        def _():
+            combine_cores(1, ch - 2)
+
+    forward_step(0)
+    span(1, CHUNKS, forward_both)
+    normalize_partner(CHUNKS - 1)
+    if CHUNKS > 1:
+        combine_cores(1, CHUNKS - 2)
+    combine_cores(1, CHUNKS - 1)
 
     def gradients(h):
         short = gs[h]
@@ -275,20 +309,14 @@
         kpart[h] = dot(mixed, q[:, cols(h)], TN)
         intra[h] = dot(sb[h], short, TN)
 
-    def gradients_own(i):
-        gradients(c * half + 2 * i)
-        gradients(c * half + 2 * i + 1)
-
-    def gradients_partner(i):
-        gradients((1 - c) * half + 2 * i)
-        gradients((1 - c) * half + 2 * i + 1)
-
-    each(half // 4, gradients_own)
-    chunked(lambda ch: combine_cores(1, ch))
-    lax.fori_loop(half // 4, half // 2, lambda i, _: (gradients_own(i), 0)[1], 0)
-    chunked(lambda ch: chain(1, ch))
-    each(half // 2, gradients_partner)
-    out_copies[1].start()
+    def gradients_pair(i):
+        gradients(2 * i)
+        gradients(2 * i + 1)
+
+    early = jnp.where(has_after, half, 2)
+    span(0, early, gradients_pair)
+    relay_all(1, has_before)
+    span(early, half, gradients_pair)
 
     def finish(h):
         fading = jnp.exp(total(0, h) - colb[h])
@@ -305,10 +333,17 @@
         for i in range(per):
             finish((1 - c) * half + ch * per + i)
 
-    chunked(finish_own)
-    chunked(finish_partner)
-    out_copies[2].start()
-    out_copies[3].start()
+    def backward_step(ch):
+        arrive(1, ch, has_before)
+        finish_own(ch)
+
+    def backward_both(ch):
+        backward_step(ch)
+        finish_partner(ch - 1)
+
+    backward_step(0)
+    span(1, CHUNKS, backward_both)
+    finish_partner(CHUNKS - 1)
 
     for i in range(3):
         total_copy(i).wait_send()
@@ -321,10 +356,20 @@
 
             @pl.when(has_after if d == 0 else has_before)
             def _():
-                move3(d, ch).wait_send()
+                for i in range(per):
+                    move3(d, ch * per + i).wait_send()
 
         chunked(drain)
-    for copy in out_copies:
+
+
+def write_out(a0, a1, a2, a3, b0, b1, b2, b3, sem):
+    copies = [
+        pltpu.make_async_copy(a, b, sem.at[i])
+        for i, (a, b) in enumerate(((a0, b0), (a1, b1), (a2, b2), (a3, b3)))
+    ]
+    for copy in copies:
+        copy.start()
+    for copy in copies:
         copy.wait()
 
 
@@ -335,14 +380,17 @@
     wire = BF16 if groups <= 8 else F32
     array = jax.ShapeDtypeStruct((rows, width), BF16)
     any_spec = pl.BlockSpec(memory_space=pl.ANY)
+    hbm_spec = pl.BlockSpec(memory_space=pltpu.HBM)
     moved = pltpu.VMEM((2, half, DH, DH), wire)
-    return pl.pallas_call(
+    vmem_spec = pl.BlockSpec(memory_space=pltpu.VMEM)
+    results = pl.pallas_call(
         functools.partial(kernel, groups, heads),
-        out_shape=(array,) * 4,
-        in_specs=[any_spec] * 4 + [pl.BlockSpec(memory_space=pltpu.VMEM)],
-        out_specs=(any_spec,) * 4,
-        scratch_shapes=[pltpu.VMEM((rows, width), BF16)] * 8
+        out_shape=(pltpu.VMEM((rows, width), BF16),) * 4,
+        in_specs=[hbm_spec] * 5,
+        out_specs=(vmem_spec,) * 4,
+        scratch_shapes=[pltpu.VMEM((rows, width), BF16)] * 4
         + [
+            pltpu.VMEM(log_decay.shape, BF16),
             pltpu.VMEM((heads, rows, DH), F32),
             pltpu.VMEM((heads, rows), F32),
             pltpu.VMEM((rows, rows), F32),
@@ -358,10 +406,9 @@
         + [moved] * 7
         + [
             pltpu.VMEM((2, heads, DH, DH), wire),
-            pltpu.SemaphoreType.DMA((4,)),
-            pltpu.SemaphoreType.DMA((4,)),
-            pltpu.SemaphoreType.DMA((4, 2, CHUNKS)),
-            pltpu.SemaphoreType.DMA((4, 2, CHUNKS)),
+            pltpu.SemaphoreType.DMA((5,)),
+            pltpu.SemaphoreType.DMA((4, 2, half)),
+            pltpu.SemaphoreType.DMA((4, 2, half)),
             pltpu.SemaphoreType.DMA((3,)),
             pltpu.SemaphoreType.DMA((3,)),
         ],
@@ -369,6 +416,14 @@
             collective_id=0, has_side_effects=True, vmem_limit_bytes=52 * 1024 * 1024
         ),
     )(queries, keys, values, out_grad, log_decay)
+    return pl.pallas_call(
+        write_out,
+        out_shape=(array,) * 4,
+        in_specs=[any_spec] * 4,
+        out_specs=(hbm_spec,) * 4,
+        scratch_shapes=[pltpu.SemaphoreType.DMA((4,))],
+        compiler_params=pltpu.CompilerParams(vmem_limit_bytes=1024 * 1024),
+    )(*results)
 
 
 def solution(mesh):

time: 62.5 us -> 50.2 us (0.80)
  Pallas kernels: 55 us -> 47.7 us
  local copies, waits for them, and re-layouts: 6.59 us -> 1.43 us
    pallas_call x1 -> x2, Pallas kernels: 55 us -> 47.7 us  [the longest x1 45.7 us: body(): pl.pallas_call(functools.partial(kernel, groups, heads), out_shape=(pltpu...]
    unnamed x11 -> x1, local copies, waits for them, and re-layouts: 6.59 us -> 1.43 us
where the time goes in v2:
time: 50.2 us; the launch traced here: 49.8 us
  Pallas kernels  47.7 us (95%)
  local copies, waits for them, and re-layouts  1.43 us (3%)
  between operations  0.64 us (1%)
    pallas_call x1, Pallas kernels, body(): pl.pallas_call(functools.partial(kernel, groups, heads), out_shape=(pltpu...  45.7 us
    pallas_call x1, Pallas kernels, body(): pl.pallas_call(write_out, out_shape=(array,) * 4, in_specs=[any_spec] * 4...  2.04 us
    unnamed x1, local copies, waits for them, and re-layouts  1.43 us

profile of v2, /device:TPU:0, one launch (start us, length us, event | category | flops | bytes accessed | tf_op | source)
XLA Modules:
  0.0 49.8 jit_solution(7751409490784142345)
XLA Ops:
  0.6 1.4 %copy.9.ld_hbm = bf16[256,16]{1,0:T(8,128)(2,1)} copy(bf16[256,16]{0,1:T(8,128)(2,1)} %param.9) | data formatting | bytes 16384 | tf_op args[4]
  2.1 45.7 %shard_map.84 = (bf16[256,2048]{1,0:T(8,128)(2,1)S(1)}, bf16[256,2048]{1,0:T(8,128)(2,1)S(1)}, bf16[256,2048]{1,0:T(8,128)(2,1)S(1)}, bf16[256,2048]{1,0:T(8,128)(2,1)S(1)}) custom-call(bf16[256,2048]{1,0:T(8,128)(2,1)} %q_hbm.1, bf16[256,2048]{1,0:T(8,128)(2,1)} %k_hbm.1, bf16[256,2048]{1,0:T(8,128)(2,1)} %v_hbm.1, bf16[256,2048]{1,0:T(8,128)(2,1)} %g_hbm.1, ...), custom_call_target="tpu_custom_call" | custom-call | tf_op jit(solution)/shard_map/pallas_call | solution.py:386
  47.8 2.0 %shard_map.85 = (bf16[256,2048]{1,0:T(8,128)(2,1)}, bf16[256,2048]{1,0:T(8,128)(2,1)}, bf16[256,2048]{1,0:T(8,128)(2,1)}, bf16[256,2048]{1,0:T(8,128)(2,1)}) custom-call(bf16[256,2048]{1,0:T(8,128)(2,1)S(1)} %get-tuple-element.8.a0, bf16[256,2048]{1,0:T(8,128)(2,1)S(1)} %get-tuple-element.9.a1, bf16[256,2048]{1,0:T(8,128)(2,1)S(1)} %get-tuple-element.10.a2, ...), custom_call_target="tpu_custom_call" | custom-call | tf_op jit(solution)/shard_map/pallas_call | solution.py:419
